TPU v7x, 32 devices: a whole 2x2x4 slice. The times are simulated.
32 devices in a mesh: row: 4 (over z), col: 4 (over x, core), dp: 2 (over y).
Axes of the slice: x: 2, y: 2, z: 4, core: 2. Of those that a mesh axis runs over, the one named last changes fastest.
Arguments:
- tokens: bfloat16 [1024, 8192], P(('dp', 'row'), 'col'), may hold values from -6 to 6
- w_in: bfloat16 [8192, 14336], P('col', 'row'), may hold values from -0.0625 to 0.0625
- w_out: bfloat16 [14336, 8192], P('row', 'col'), may hold values from -0.046875 to 0.046875
- spike_gain: float32 [14336], P('row'), may hold values from 1 to 4
- cotangent: bfloat16 [1024, 8192], P(('dp', 'row'), 'col'), may hold values from -1.5 to 1.5
Outputs:
- output: bfloat16 [1024, 8192], P(('dp', 'row'), 'col')
- grad_tokens: bfloat16 [1024, 8192], P(('dp', 'row'), 'col')
- grad_w_in: bfloat16 [8192, 14336], P('col', 'row')
- grad_w_out: bfloat16 [14336, 8192], P('row', 'col')
All inputs are finite; a program needn't handle non-finite values.
Results may differ from a plain program's by a relative error of at most 0.035.
Values may be sent and summed in bfloat16 or wider, within the bound.
No kernel may reach another device: no remote copies, remote signals or barrier semaphores. Data moves between devices by JAX's collectives and lax.ppermute only.
A program may use at most 192 MiB of HBM per device.

v0:
```python
import jax
import jax.numpy as jnp
from jax import lax
from jax.sharding import PartitionSpec as P

LEVELS = 4


sharpness = 4.0


def spike_parts(potential, gain):
    scaled = potential * gain[None, :]
    total = jnp.zeros_like(scaled)
    slope = jnp.zeros_like(scaled)
    for level in range(LEVELS):
        sig = jax.nn.sigmoid(sharpness * (scaled - (level + 0.5)))
        total = total + sig
        slope = slope + sig * (1.0 - sig)
    return (total, slope * (sharpness * gain[None, :]))


def times_transposed(left, right):
    return lax.dot_general(
        left, right, (((1,), (1,)), ((), ())), preferred_element_type=jnp.float32
    )


def over_tokens(left, right):
    return lax.dot_general(
        left, right, (((0,), (0,)), ((), ())), preferred_element_type=jnp.float32
    )


def shards(tokens, w_in, w_out, spike_gain, cotangent):
    tok_all = lax.all_gather(tokens, "row", axis=0, tiled=True)
    potential = lax.psum_scatter(
        jnp.dot(tok_all, w_in, preferred_element_type=jnp.float32).astype(jnp.bfloat16),
        "col",
        scatter_dimension=0,
        tiled=True,
    ).astype(jnp.float32)
    total, slope = spike_parts(potential, spike_gain)
    spikes = total.astype(jnp.bfloat16)
    spike_all = lax.all_gather(spikes, "col", axis=0, tiled=True)
    output = lax.psum_scatter(
        jnp.dot(spike_all, w_out, preferred_element_type=jnp.float32).astype(jnp.bfloat16),
        "row",
        scatter_dimension=0,
        tiled=True,
    )
    cot_all = lax.all_gather(cotangent, "row", axis=0, tiled=True)
    grad_spikes = lax.psum_scatter(
        times_transposed(cot_all, w_out).astype(jnp.bfloat16),
        "col",
        scatter_dimension=0,
        tiled=True,
    ).astype(jnp.float32)
    grad_potential = (grad_spikes * slope).astype(jnp.bfloat16)
    grad_all = lax.all_gather(grad_potential, "col", axis=0, tiled=True)
    grad_tokens = lax.psum_scatter(
        times_transposed(grad_all, w_in).astype(jnp.bfloat16),
        "row",
        scatter_dimension=0,
        tiled=True,
    )
    grad_w_in = over_tokens(tok_all, grad_all)
    grad_w_out = over_tokens(spike_all, cot_all)
    grad_w_in, grad_w_out = (
        lax.psum(grad_w_in.astype(jnp.bfloat16), "dp").astype(jnp.float32),
        lax.psum(grad_w_out.astype(jnp.bfloat16), "dp").astype(jnp.float32),
    )
    return (output, grad_tokens, grad_w_in.astype(jnp.bfloat16), grad_w_out.astype(jnp.bfloat16))


def solution(mesh):
    placed = (
        P(("dp", "row"), "col"),
        P("col", "row"),
        P("row", "col"),
        P("row"),
        P(("dp", "row"), "col"),
    )
    return jax.shard_map(
        shards,
        mesh=mesh,
        in_specs=placed,
        out_specs=(
            P(("dp", "row"), "col"),
            P(("dp", "row"), "col"),
            P("col", "row"),
            P("row", "col"),
        ),
        check_vma=False,
    )
```

profile of v0, /device:TPU:0, one launch (start us, length us, event | category | flops | bytes accessed | tf_op | source)
XLA Modules:
  0.0 1037.4 jit_solution(3584940277076545059)
XLA Ops:
  7.2 0.0 all-gather.9.cloned.1.call-start
  7.2 0.7 all-gather.9.cloned.1.call-update
  7.9 0.0 all-gather.5.cloned.1.call-start
  7.9 0.7 all-gather.5.cloned.1.call-update
  8.6 0.0 reduce-scatter.9.cloned.1.call-start
  8.7 49.5 %all-gather.9.cloned.1.call-done = bf16[512,2048]{1,0:T(8,128)(2,1)} async-done(((bf16[128,2048]{1,0:T(8,128)(2,1)}), bf16[512,2048]{1,0:T(8,128)(2,1)}) %all-gather.9.cloned.1.call-update) | async-done | bytes 2097168 | tf_op jit(solution)/shard_map/all_gather | solution.py:52
  58.2 12.9 %convolution_convert_fusion.2 = bf16[512,3584]{1,0:T(8,128)(2,1)} fusion(bf16[512,2048]{1,0:T(8,128)(2,1)} %all-gather.9.cloned.1.call-done, bf16[3584,2048]{1,0:T(8,128)(2,1)} %param.7), kind=kOutput, calls=%fused_computation.3 | convolution fusion | flops 7518027776 | bytes 20447232 | tf_op jit(solution)/shard_map/dot_general | solution.py:24
  71.2 0.0 reduce-scatter.5.cloned.1.call-start
  71.2 33.2 %all-gather.5.cloned.1.call-done = bf16[512,2048]{1,0:T(8,128)(2,1)} async-done(((bf16[128,2048]{1,0:T(8,128)(2,1)}), bf16[512,2048]{1,0:T(8,128)(2,1)}) %all-gather.5.cloned.1.call-update) | async-done | bytes 2097168 | tf_op jit(solution)/shard_map/all_gather | solution.py:36
  104.5 12.8 %convolution_convert_fusion.3 = bf16[512,3584]{1,0:T(8,128)(2,1)} fusion(bf16[512,2048]{1,0:T(8,128)(2,1)} %all-gather.5.cloned.1.call-done, bf16[2048,3584]{1,0:T(8,128)(2,1)} %param.6), kind=kOutput, calls=%fused_computation.4 | convolution fusion | flops 7518027776 | bytes 20447232 | tf_op jit(solution)/shard_map/dot_general | solution.py:38
  117.3 0.0 all-gather.11.cloned.1.call-start
  117.4 0.6 copy-done
  118.0 29.6 %reduce-scatter.9.cloned.1.call-done = bf16[128,3584]{1,0:T(8,128)(2,1)} async-done(((bf16[512,3584]{1,0:T(8,128)(2,1)}), bf16[128,3584]{1,0:T(8,128)(2,1)}) %reduce-scatter.9.cloned.1.call-update) | async-done | bytes 917520 | tf_op jit(solution)/shard_map/reduce_scatter | solution.py:53
  147.6 44.4 %reduce-scatter.5.cloned.1.call-done = bf16[128,3584]{1,0:T(8,128)(2,1)} async-done(((bf16[512,3584]{1,0:T(8,128)(2,1)}), bf16[128,3584]{1,0:T(8,128)(2,1)}) %reduce-scatter.5.cloned.1.call-update) | async-done | bytes 917520 | tf_op jit(solution)/shard_map/reduce_scatter | solution.py:37
  192.0 4.7 fusion.6
  196.7 0.0 all-gather.11.cloned.1.call-update
  196.7 0.0 all-gather.7.cloned.1.call-start
  196.8 0.5 all-gather.7.cloned.1.call-update
  197.3 0.2 all-reduce.3.cloned.1.call-start
  197.6 30.9 %all-gather.11.cloned.1.call-done = bf16[512,3584]{1,0:T(8,128)(2,1)} async-done(((bf16[128,3584]{1,0:T(8,128)(2,1)}), bf16[512,3584]{1,0:T(8,128)(2,1)}) %all-gather.11.cloned.1.call-update) | async-done | bytes 3670032 | tf_op jit(solution)/shard_map/all_gather | solution.py:60
  228.4 13.2 %fusion = bf16[2048,3584]{0,1:T(8,128)(2,1)} fusion(bf16[512,3584]{1,0:T(8,128)(2,1)} %all-gather.11.cloned.1.call-done, bf16[512,2048]{1,0:T(8,128)(2,1)} %all-gather.5.cloned.1.call-done), kind=kOutput, calls=%fused_computation.2 | convolution fusion | flops 7523532800 | bytes 20447232 | tf_op jit(solution)/shard_map/dot_general | solution.py:30
  241.7 20.3 %all-gather.7.cloned.1.call-done = bf16[512,3584]{1,0:T(8,128)(2,1)} async-done(((bf16[128,3584]{1,0:T(8,128)(2,1)}), bf16[512,3584]{1,0:T(8,128)(2,1)}) %all-gather.7.cloned.1.call-update) | async-done | bytes 3670032 | tf_op jit(solution)/shard_map/all_gather | solution.py:45
  262.0 13.1 %convolution_convert_fusion = bf16[3584,2048]{1,0:T(8,128)(2,1)} fusion(bf16[512,3584]{1,0:T(8,128)(2,1)} %all-gather.7.cloned.1.call-done, bf16[512,2048]{1,0:T(8,128)(2,1)S(1)} %copy-done.1), kind=kOutput, calls=%fused_computation | convolution fusion | flops 7523532800 | bytes 20447232 | tf_op jit(solution)/shard_map/dot_general | solution.py:30
  275.1 0.0 reduce-scatter.7.cloned.1.call-start
  275.2 13.1 %convolution_convert_fusion.5 = bf16[512,2048]{1,0:T(8,128)(2,1)} fusion(bf16[512,3584]{1,0:T(8,128)(2,1)} %all-gather.7.cloned.1.call-done, bf16[3584,2048]{1,0:T(8,128)(2,1)} %param.7), kind=kOutput, calls=%fused_computation.6 | convolution fusion | flops 7517241344 | bytes 20447232 | tf_op jit(solution)/shard_map/dot_general | solution.py:47
  288.3 0.3 reduce-scatter.11.cloned.1.call-start
  288.6 13.1 %convolution_convert_fusion.4 = bf16[512,2048]{1,0:T(8,128)(2,1)} fusion(bf16[512,3584]{1,0:T(8,128)(2,1)} %all-gather.11.cloned.1.call-done, bf16[2048,3584]{1,0:T(8,128)(2,1)} %param.6), kind=kOutput, calls=%fused_computation.5 | convolution fusion | flops 7517241344 | bytes 20447232 | tf_op jit(solution)/shard_map/dot_general | solution.py:24
  301.7 622.7 %all-reduce.3.cloned.1.call-done = (bf16[2048,3584]{0,1:T(8,128)(2,1)}, bf16[3584,2048]{1,0:T(8,128)(2,1)}) async-done(((bf16[2048,3584]{0,1:T(8,128)(2,1)}, bf16[3584,2048]{1,0:T(8,128)(2,1)}), (bf16[2048,3584]{0,1:T(8,128)(2,1)}, bf16[3584,2048]{1,0:T(8,128)(2,1)})) %all-reduce.3.cloned.1.call-update) | async-done | bytes 29360144 | tf_op jit(solution)/shard_map/psum | solution.py:70
  924.4 18.7 %copy.9 = bf16[2048,3584]{1,0:T(8,128)(2,1)} copy(bf16[2048,3584]{0,1:T(8,128)(2,1)} %get-tuple-element.8) | data formatting | bytes 29360128
  943.1 28.1 %reduce-scatter.7.cloned.1.call-done = bf16[128,2048]{1,0:T(8,128)(2,1)} async-done(((bf16[512,2048]{1,0:T(8,128)(2,1)}), bf16[128,2048]{1,0:T(8,128)(2,1)}) %reduce-scatter.7.cloned.1.call-update) | async-done | bytes 524304 | tf_op jit(solution)/shard_map/reduce_scatter | solution.py:46
  971.2 46.2 %reduce-scatter.11.cloned.1.call-done = bf16[128,2048]{1,0:T(8,128)(2,1)} async-done(((bf16[512,2048]{1,0:T(8,128)(2,1)}), bf16[128,2048]{1,0:T(8,128)(2,1)}) %reduce-scatter.11.cloned.1.call-update) | async-done | bytes 524304 | tf_op jit(solution)/shard_map/reduce_scatter | solution.py:61
  1017.4 13.5 %copy.12 = bf16[3584,2048]{1,0:T(8,128)(2,1)} copy(bf16[3584,2048]{1,0:T(8,128)(2,1)} %get-tuple-element.15) | data formatting | bytes 29360128
  (9 shorter events, 0.1 us)
Async XLA Ops:
  7.2 51.1 %all-gather.9.cloned.1.call-start = ((), (), s32[]{:S(2)}) async-start(), calls=%async_computation.8 | async-start | bytes 2621440 | tf_op jit(solution)/shard_map/all_gather | solution.py:52
  7.9 96.6 %all-gather.5.cloned.1.call-start = ((), (), s32[]{:S(2)}) async-start(), calls=%async_computation.4 | async-start | bytes 2621440 | tf_op jit(solution)/shard_map/all_gather | solution.py:36
  8.6 138.9 %reduce-scatter.9.cloned.1.call-start = ((), (), s32[]{:S(2)}) async-start(), calls=%async_computation.9 | async-start | bytes 4587520 | tf_op jit(solution)/shard_map/reduce_scatter | solution.py:53
  71.2 120.8 %reduce-scatter.5.cloned.1.call-start = ((), (), s32[]{:S(2)}) async-start(), calls=%async_computation.5 | async-start | bytes 4587520 | tf_op jit(solution)/shard_map/reduce_scatter | solution.py:37
  117.3 0.7 copy-start
  117.3 111.1 %all-gather.11.cloned.1.call-start = ((), (), s32[]{:S(2)}) async-start(), calls=%async_computation.10 | async-start | bytes 4587520 | tf_op jit(solution)/shard_map/all_gather | solution.py:60
  196.7 65.2 %all-gather.7.cloned.1.call-start = ((), (), s32[]{:S(2)}) async-start(), calls=%async_computation.6 | async-start | bytes 4587520 | tf_op jit(solution)/shard_map/all_gather | solution.py:45
  197.3 64.6 %copy-start.1 = (bf16[512,2048]{1,0:T(8,128)(2,1)S(1)}, bf16[512,2048]{1,0:T(8,128)(2,1)}, u32[]{:S(2)}) copy-start(bf16[512,2048]{1,0:T(8,128)(2,1)} %all-gather.9.cloned.1.call-done) | copy-start | bytes 6291460
  197.3 727.1 %all-reduce.3.cloned.1.call-start = ((), (), s32[]{:S(2)}) async-start(), calls=%async_computation.12 | async-start | bytes 58720256 | tf_op jit(solution)/shard_map/psum | solution.py:70
  275.1 696.1 %reduce-scatter.7.cloned.1.call-start = ((), (), s32[]{:S(2)}) async-start(), calls=%async_computation.7 | async-start | bytes 2621440 | tf_op jit(solution)/shard_map/reduce_scatter | solution.py:46
  288.3 729.1 %reduce-scatter.11.cloned.1.call-start = ((), (), s32[]{:S(2)}) async-start(), calls=%async_computation.11 | async-start | bytes 2621440 | tf_op jit(solution)/shard_map/reduce_scatter | solution.py:61
Sparse Core Ops, SparseCore 0:
  9.6 48.6 all-gather.8
  59.8 44.6 all-gather.4
  107.6 39.9 reduce-scatter.8
  150.7 41.2 reduce-scatter.4
  196.9 31.5 all-gather.10
  230.4 31.4 all-gather.6
  275.2 649.1 all-reduce.2
  927.3 43.8 reduce-scatter.6
  974.1 43.1 reduce-scatter.10
where the time goes:
time: 1040 us
  waiting for transfers between devices  907 us (87%)
  matrix products  78.4 us (8%)
  local copies, waits for them, and re-layouts  32.8 us (3%)
  between operations  13.9 us (1%)
    psum x1, waiting for transfers between devices, shards(): lax.psum(grad_w_in.astype(jnp.bfloat16), 'dp').astype(jnp.float32)  623 us
    all_gather x1, waiting for transfers between devices, shards(): cot_all = lax.all_gather(cotangent, 'row', axis=0, tiled=True)  49.5 us
    reduce_scatter x1, waiting for transfers between devices, shards(): lax.psum_scatter(times_transposed(grad_all, w_in).astype(jnp.bfloat16), '...  46.2 us
    reduce_scatter x1, waiting for transfers between devices, shards(): lax.psum_scatter(jnp.dot(tok_all, w_in, preferred_element_type=jnp.float3...  44.4 us
    all_gather x1, waiting for transfers between devices, shards(): tok_all = lax.all_gather(tokens, 'row', axis=0, tiled=True)  33.2 us
    unnamed x6, local copies, waits for them, and re-layouts  32.8 us
    all_gather x1, waiting for transfers between devices, shards(): grad_all = lax.all_gather(grad_potential, 'col', axis=0, tiled=True)  30.9 us
    reduce_scatter x1, waiting for transfers between devices, shards(): lax.psum_scatter(times_transposed(cot_all, w_out).astype(jnp.bfloat16), '...  29.6 us
  transfers between devices with their start and end apart: 9, of which 9 were waited for; matrix products, arithmetic and copies ran while one was open for 8% of the time, Pallas kernels for 0%

commit v1 on v0

v1 whole, which is shorter than its diff:
```python
import jax
import jax.numpy as jnp
from jax import lax
from jax.sharding import PartitionSpec as P

LEVELS = 4


sharpness = 4.0


def spike_parts(potential, gain):
    scaled = potential * gain[None, :]
    total = jnp.zeros_like(scaled)
    slope = jnp.zeros_like(scaled)
    for level in range(LEVELS):
        sig = jax.nn.sigmoid(sharpness * (scaled - (level + 0.5)))
        total = total + sig
        slope = slope + sig * (1.0 - sig)
    return (total, slope * (sharpness * gain[None, :]))


def times_transposed(left, right):
    return lax.dot_general(
        left, right, (((1,), (1,)), ((), ())), preferred_element_type=jnp.float32
    )


def over_tokens(left, right):
    return lax.dot_general(
        left, right, (((0,), (0,)), ((), ())), preferred_element_type=jnp.float32
    )


def from_other_halves(value, n_dp):
    return [
        lax.ppermute(value, "dp", [(d, (d + k) % n_dp) for d in range(n_dp)])
        for k in range(1, n_dp)
    ]


def shards(n_dp, tokens, w_in, w_out, spike_gain, cotangent):
    def gathered(value, axis):
        return lax.all_gather(value, axis, axis=0, tiled=True)

    def scattered(value, axis):
        return lax.psum_scatter(
            value.astype(jnp.bfloat16), axis, scatter_dimension=0, tiled=True
        )

    tok_all = gathered(tokens, "row")
    potential = scattered(
        jnp.dot(tok_all, w_in, preferred_element_type=jnp.float32), "col"
    ).astype(jnp.float32)
    cot_all = gathered(cotangent, "row")
    grad_spikes = scattered(times_transposed(cot_all, w_out), "col").astype(jnp.float32)
    total, slope = spike_parts(potential, spike_gain)
    spikes = total.astype(jnp.bfloat16)
    spike_all = gathered(spikes, "col")
    output = scattered(
        jnp.dot(spike_all, w_out, preferred_element_type=jnp.float32), "row"
    )
    grad_potential = (grad_spikes * slope).astype(jnp.bfloat16)
    grad_all = gathered(grad_potential, "col")
    grad_tokens = scattered(times_transposed(grad_all, w_in), "row")

    def every_half(own, others):
        return jnp.concatenate([own] + others, axis=0)

    tok_every = every_half(tok_all, from_other_halves(tok_all, n_dp))
    cot_every = every_half(cot_all, from_other_halves(cot_all, n_dp))
    spike_every = every_half(
        spike_all, [gathered(part, "col") for part in from_other_halves(spikes, n_dp)]
    )
    grad_every = every_half(
        grad_all,
        [gathered(part, "col") for part in from_other_halves(grad_potential, n_dp)],
    )
    grad_w_out = over_tokens(spike_every, cot_every).astype(jnp.bfloat16)
    grad_w_in = over_tokens(tok_every, grad_every).astype(jnp.bfloat16)
    return (output, grad_tokens, grad_w_in, grad_w_out)


def solution(mesh):
    placed = (
        P(("dp", "row"), "col"),
        P("col", "row"),
        P("row", "col"),
        P("row"),
        P(("dp", "row"), "col"),
    )

    def program(*args):
        return shards(mesh.shape["dp"], *args)

    return jax.shard_map(
        program,
        mesh=mesh,
        in_specs=placed,
        out_specs=(
            P(("dp", "row"), "col"),
            P(("dp", "row"), "col"),
            P("col", "row"),
            P("row", "col"),
        ),
        check_vma=False,
    )
```

time: 1040 us -> 428 us (0.41)
  waiting for transfers between devices: 907 us -> 305 us
  local copies, waits for them, and re-layouts: 32.8 us -> 2.57 us
  matrix products: 78.4 us -> 95.9 us
    psum x1 -> x0, waiting for transfers between devices: 623 us -> none  [shards(): lax.psum(grad_w_in.astype(jnp.bfloat16), 'dp').astype(jnp.float32)]
    ppermute x0 -> x4, waiting for transfers between devices: none -> 91.6 us  [from_other_halves(): lax.ppermute(value, 'dp', [(d, (d + k) % n_dp) for d in range(n_dp)])]
    all_gather x4 -> x6, waiting for transfers between devices: 134 us -> 85.7 us  [gathered(): return lax.all_gather(value, axis, axis=0, tiled=True)]
    unnamed x6 -> x8, local copies, waits for them, and re-layouts: 32.8 us -> 2.57 us
    reduce_scatter x4, waiting for transfers between devices: 148 us -> 125 us  [scattered(): lax.psum_scatter(value.astype(jnp.bfloat16), axis, scatter_dimension=0, t...]
    dot_general x2, matrix products: 26.4 us -> 43.7 us  [over_tokens(): lax.dot_general(left, right, (((0,), (0,)), ((), ())), preferred_element_...]
  transfers between devices with their start and end apart: 9 -> 14, of which waited for: 9 -> 11; matrix products, arithmetic and copies ran while one was open for 8% -> 22% of each run, Pallas kernels for 0% -> 0%
where the time goes in v1:
time: 428 us
  waiting for transfers between devices  305 us (71%)
  matrix products  95.9 us (22%)
  between operations  14.2 us (3%)
  starting transfers between devices  5.75 us (1%)
  other arithmetic  4.71 us (1%)
    reduce_scatter x4, waiting for transfers between devices, scattered(): lax.psum_scatter(value.astype(jnp.bfloat16), axis, scatter_dimension=0, t...  125 us
    ppermute x4, waiting for transfers between devices, from_other_halves(): lax.ppermute(value, 'dp', [(d, (d + k) % n_dp) for d in range(n_dp)])  91.6 us
    all_gather x6, waiting for transfers between devices, gathered(): return lax.all_gather(value, axis, axis=0, tiled=True)  85.7 us
    dot_general x2, matrix products, over_tokens(): lax.dot_general(left, right, (((0,), (0,)), ((), ())), preferred_element_...  43.7 us
    dot_general x2, matrix products, times_transposed(): lax.dot_general(left, right, (((1,), (1,)), ((), ())), preferred_element_...  26 us
    dot_general x1, matrix products, shards(): jnp.dot(spike_all, w_out, preferred_element_type=jnp.float32)  13.3 us
    dot_general x1, matrix products, shards(): jnp.dot(tok_all, w_in, preferred_element_type=jnp.float32)  12.9 us
  transfers between devices with their start and end apart: 14, of which 11 were waited for; matrix products, arithmetic and copies ran while one was open for 22% of the time, Pallas kernels for 0%

profile of v1, /device:TPU:0, one launch (start us, length us, event | category | flops | bytes accessed | tf_op | source)
XLA Modules:
  0.0 427.8 jit_solution(13461405699323162961)
XLA Ops:
  7.2 0.7 all-gather.11.cloned.1.call-update
  7.9 0.7 all-gather.7.cloned.1.call-update
  8.7 49.5 %all-gather.11.cloned.1.call-done = bf16[512,2048]{1,0:T(8,128)(2,1)} async-done(((bf16[128,2048]{1,0:T(8,128)(2,1)}), bf16[512,2048]{1,0:T(8,128)(2,1)}) %all-gather.11.cloned.1.call-update) | async-done | bytes 2097168 | tf_op jit(solution)/shard_map/all_gather | solution.py:44
  58.2 12.9 %convolution_convert_fusion.2 = bf16[512,3584]{1,0:T(8,128)(2,1)} fusion(bf16[512,2048]{1,0:T(8,128)(2,1)} %all-gather.11.cloned.1.call-done, bf16[3584,2048]{1,0:T(8,128)(2,1)} %param.7), kind=kOutput, calls=%fused_computation.8 | convolution fusion | flops 7518027776 | bytes 20447232 | tf_op jit(solution)/shard_map/dot_general | solution.py:24
  71.2 0.0 reduce-scatter.5.cloned.1.call-start
  71.2 33.2 %all-gather.7.cloned.1.call-done = bf16[512,2048]{1,0:T(8,128)(2,1)} async-done(((bf16[128,2048]{1,0:T(8,128)(2,1)}), bf16[512,2048]{1,0:T(8,128)(2,1)}) %all-gather.7.cloned.1.call-update) | async-done | bytes 2097168 | tf_op jit(solution)/shard_map/all_gather | solution.py:44
  104.5 12.9 %convolution_convert_fusion.3 = bf16[512,3584]{1,0:T(8,128)(2,1)} fusion(bf16[512,2048]{1,0:T(8,128)(2,1)} %all-gather.7.cloned.1.call-done, bf16[2048,3584]{1,0:T(8,128)(2,1)} %param.6), kind=kOutput, calls=%fused_computation.9 | convolution fusion | flops 7518027776 | bytes 20447232 | tf_op jit(solution)/shard_map/dot_general | solution.py:53
  117.4 0.0 all-gather.9.cloned.1.call-start
  117.5 0.6 copy-done.2
  118.1 29.5 %reduce-scatter.9.cloned.1.call-done = bf16[128,3584]{1,0:T(8,128)(2,1)} async-done(((bf16[512,3584]{1,0:T(8,128)(2,1)}), bf16[128,3584]{1,0:T(8,128)(2,1)}) %reduce-scatter.9.cloned.1.call-update) | async-done | bytes 917520 | tf_op jit(solution)/shard_map/reduce_scatter | solution.py:47
  147.6 44.4 %reduce-scatter.5.cloned.1.call-done = bf16[128,3584]{1,0:T(8,128)(2,1)} async-done(((bf16[512,3584]{1,0:T(8,128)(2,1)}), bf16[128,3584]{1,0:T(8,128)(2,1)}) %reduce-scatter.5.cloned.1.call-update) | async-done | bytes 917520 | tf_op jit(solution)/shard_map/reduce_scatter | solution.py:47
  192.0 4.7 %fusion.17 = (bf16[128,3584]{1,0:T(8,128)(2,1)}, bf16[128,3584]{1,0:T(8,128)(2,1)}) fusion(bf16[128,3584]{1,0:T(8,128)(2,1)} %reduce-scatter.9.cloned.1.call-done, f32[3584]{0:T(1024)S(1)} %broadcast_multiply_fusion, f32[3584]{0:T(1024)S(1)} %copy-done.2, bf16[128,3584]{1,0:T(8,128)(2,1)} %reduce-scatter.5.cloned.1.call-done), kind=kLoop, calls=%fused_computation.27 | loop fusion | flops 18808832 | bytes 3698688 | tf_op jit(solution)/shard_map/convert_element_type | solution.py:63
  196.8 0.0 all-gather.13.cloned.1.call-start
  196.8 0.5 all-gather.13.cloned.1.call-update
  197.4 1.5 collective-permute-start.1
  198.9 20.8 %collective-permute-done.1 = bf16[128,3584]{1,0:T(8,128)(2,1)S(1)} collective-permute-done((bf16[128,3584]{1,0:T(8,128)(2,1)}, bf16[128,3584]{1,0:T(8,128)(2,1)S(1)}, u32[]{:S(2)}, u32[]{:S(2)}) %collective-permute-start.1) | collective-permute-done | bytes 917536 | tf_op jit(solution)/shard_map/ppermute | solution.py:37
  219.8 0.9 copy-done
  220.7 1.5 collective-permute-start.2
  222.3 20.1 %collective-permute-done.2 = bf16[128,3584]{1,0:T(8,128)(2,1)S(1)} collective-permute-done((bf16[128,3584]{1,0:T(8,128)(2,1)}, bf16[128,3584]{1,0:T(8,128)(2,1)S(1)}, u32[]{:S(2)}, u32[]{:S(2)}) %collective-permute-start.2) | collective-permute-done | bytes 917536 | tf_op jit(solution)/shard_map/ppermute | solution.py:37
  242.3 1.0 copy-done.1
  243.5 13.3 %convolution_convert_fusion.5 = bf16[512,2048]{1,0:T(8,128)(2,1)} fusion(bf16[512,3584]{1,0:T(8,128)(2,1)} %all-gather.9.cloned.1.call-done, bf16[3584,2048]{1,0:T(8,128)(2,1)} %param.7), kind=kOutput, calls=%fused_computation.17 | convolution fusion | flops 7517241344 | bytes 20447232 | tf_op jit(solution)/shard_map/dot_general | solution.py:61
  256.8 0.2 reduce-scatter.11.cloned.1.call-start
  257.0 1.5 collective-permute-start
  258.6 0.5 collective-permute-start.3
  259.1 2.9 all-gather.13.cloned.1.call-done
  262.0 13.1 %convolution_convert_fusion.4 = bf16[512,2048]{1,0:T(8,128)(2,1)} fusion(bf16[512,3584]{1,0:T(8,128)(2,1)} %all-gather.13.cloned.1.call-done, bf16[2048,3584]{1,0:T(8,128)(2,1)} %param.6), kind=kOutput, calls=%fused_computation.16 | convolution fusion | flops 7517241344 | bytes 20447232 | tf_op jit(solution)/shard_map/dot_general | solution.py:24
  275.1 30.9 %collective-permute-done = bf16[512,2048]{1,0:T(8,128)(2,1)} collective-permute-done((bf16[512,2048]{1,0:T(8,128)(2,1)}, bf16[512,2048]{1,0:T(8,128)(2,1)}, u32[]{:S(2)}, u32[]{:S(2)}) %collective-permute-start) | collective-permute-done | bytes 2097184 | tf_op jit(solution)/shard_map/ppermute | solution.py:37
  306.0 22.2 %convolution_convert_fusion.1 = bf16[2048,3584]{1,0:T(8,128)(2,1)} fusion(bf16[512,3584]{1,0:T(8,128)(2,1)} %all-gather.15.cloned.1.call-done, bf16[512,3584]{1,0:T(8,128)(2,1)} %all-gather.13.cloned.1.call-done, bf16[512,2048]{1,0:T(8,128)(2,1)} %collective-permute-done, bf16[512,2048]{1,0:T(8,128)(2,1)} %all-gather.7.cloned.1.call-done), kind=kOutput, calls=%fused_computation.1 | convolution fusion | flops 15062794240 | bytes 26214400 | tf_op jit(solution)/shard_map/dot_general | solution.py:30
  328.1 19.8 %collective-permute-done.3 = bf16[512,2048]{1,0:T(8,128)(2,1)} collective-permute-done((bf16[512,2048]{1,0:T(8,128)(2,1)S(1)}, bf16[512,2048]{1,0:T(8,128)(2,1)}, u32[]{:S(2)}, u32[]{:S(2)}) %collective-permute-start.3) | collective-permute-done | bytes 2097184 | tf_op jit(solution)/shard_map/ppermute | solution.py:37
  348.0 21.5 %convolution_convert_fusion = bf16[3584,2048]{1,0:T(8,128)(2,1)} fusion(bf16[512,3584]{1,0:T(8,128)(2,1)} %all-gather.17.cloned.1.call-done, bf16[512,3584]{1,0:T(8,128)(2,1)} %all-gather.9.cloned.1.call-done, bf16[512,2048]{1,0:T(8,128)(2,1)} %collective-permute-done.3, bf16[512,2048]{1,0:T(8,128)(2,1)S(1)} %copy-done.3), kind=kOutput, calls=%fused_computation | convolution fusion | flops 15062794240 | bytes 26214400 | tf_op jit(solution)/shard_map/dot_general | solution.py:30
  369.5 5.5 %reduce-scatter.7.cloned.1.call-done = bf16[128,2048]{1,0:T(8,128)(2,1)} async-done(((bf16[512,2048]{1,0:T(8,128)(2,1)}), bf16[128,2048]{1,0:T(8,128)(2,1)}) %reduce-scatter.7.cloned.1.call-update) | async-done | bytes 524304 | tf_op jit(solution)/shard_map/reduce_scatter | solution.py:47
  375.0 46.0 %reduce-scatter.11.cloned.1.call-done = bf16[128,2048]{1,0:T(8,128)(2,1)} async-done(((bf16[512,2048]{1,0:T(8,128)(2,1)}), bf16[128,2048]{1,0:T(8,128)(2,1)}) %reduce-scatter.11.cloned.1.call-update) | async-done | bytes 524304 | tf_op jit(solution)/shard_map/reduce_scatter | solution.py:47
  (22 shorter events, 0.4 us)
Async XLA Ops:
  7.2 51.1 %all-gather.11.cloned.1.call-start = ((), (), s32[]{:S(2)}) async-start(), calls=%async_computation.8 | async-start | bytes 2621440 | tf_op jit(solution)/shard_map/all_gather | solution.py:44
  7.9 96.6 %all-gather.7.cloned.1.call-start = ((), (), s32[]{:S(2)}) async-start(), calls=%async_computation.4 | async-start | bytes 2621440 | tf_op jit(solution)/shard_map/all_gather | solution.py:44
  8.6 139.0 %reduce-scatter.9.cloned.1.call-start = ((), (), s32[]{:S(2)}) async-start(), calls=%async_computation.9 | async-start | bytes 4587520 | tf_op jit(solution)/shard_map/reduce_scatter | solution.py:47
  71.2 120.9 %reduce-scatter.5.cloned.1.call-start = ((), (), s32[]{:S(2)}) async-start(), calls=%async_computation.5 | async-start | bytes 4587520 | tf_op jit(solution)/shard_map/reduce_scatter | solution.py:47
  117.4 0.7 copy-start.2
  117.4 126.1 %all-gather.9.cloned.1.call-start = ((), (), s32[]{:S(2)}) async-start(), calls=%async_computation.6 | async-start | bytes 4587520 | tf_op jit(solution)/shard_map/all_gather | solution.py:44
  196.8 65.2 %all-gather.13.cloned.1.call-start = ((), (), s32[]{:S(2)}) async-start(), calls=%async_computation.10 | async-start | bytes 4587520 | tf_op jit(solution)/shard_map/all_gather | solution.py:44
  197.4 108.6 %all-gather.15.cloned.1.call-start = ((), (), s32[]{:S(2)}) async-start(), calls=%async_computation.12 | async-start | bytes 4587520 | tf_op jit(solution)/shard_map/all_gather | solution.py:44
  197.4 22.4 %collective-permute-start.1 = (bf16[128,3584]{1,0:T(8,128)(2,1)}, bf16[128,3584]{1,0:T(8,128)(2,1)S(1)}, u32[]{:S(2)}, u32[]{:S(2)}) collective-permute-start(bf16[128,3584]{1,0:T(8,128)(2,1)} %get-tuple-element.4), channel_id=1, source_target_pairs={{0,1},{1,0},{2,3},{3,2},{4,5},{5,4},{6,7},{7,6},{8,9},{9,8},{10,11... | collective-permute-start | bytes 2752520 | tf_op jit(solution)/shard_map/ppermute | solution.py:37
  219.8 0.9 copy-start
  220.7 127.3 %all-gather.17.cloned.1.call-start = ((), (), s32[]{:S(2)}) async-start(), calls=%async_computation.13 | async-start | bytes 4587520 | tf_op jit(solution)/shard_map/all_gather | solution.py:44
  220.7 21.6 %collective-permute-start.2 = (bf16[128,3584]{1,0:T(8,128)(2,1)}, bf16[128,3584]{1,0:T(8,128)(2,1)S(1)}, u32[]{:S(2)}, u32[]{:S(2)}) collective-permute-start(bf16[128,3584]{1,0:T(8,128)(2,1)} %get-tuple-element.5), channel_id=1, source_target_pairs={{0,1},{1,0},{2,3},{3,2},{4,5},{5,4},{6,7},{7,6},{8,9},{9,8},{10,11... | collective-permute-start | bytes 2752520 | tf_op jit(solution)/shard_map/ppermute | solution.py:37
  242.3 1.0 copy-start.1
  243.4 15.2 %copy-start.3 = (bf16[512,2048]{1,0:T(8,128)(2,1)S(1)}, bf16[512,2048]{1,0:T(8,128)(2,1)}, u32[]{:S(2)}) copy-start(bf16[512,2048]{1,0:T(8,128)(2,1)} %all-gather.11.cloned.1.call-done) | copy-start | bytes 6291460
  243.4 131.6 %reduce-scatter.7.cloned.1.call-start = ((), (), s32[]{:S(2)}) async-start(), calls=%async_computation.7 | async-start | bytes 2621440 | tf_op jit(solution)/shard_map/reduce_scatter | solution.py:47
  256.8 164.2 %reduce-scatter.11.cloned.1.call-start = ((), (), s32[]{:S(2)}) async-start(), calls=%async_computation.11 | async-start | bytes 2621440 | tf_op jit(solution)/shard_map/reduce_scatter | solution.py:47
  257.0 49.0 %collective-permute-start = (bf16[512,2048]{1,0:T(8,128)(2,1)}, bf16[512,2048]{1,0:T(8,128)(2,1)}, u32[]{:S(2)}, u32[]{:S(2)}) collective-permute-start(bf16[512,2048]{1,0:T(8,128)(2,1)} %all-gather.7.cloned.1.call-done), channel_id=1, source_target_pairs={{0,1},{1,0},{2,3},{3,2},{4,5},{5,4},{6,7},{7,6},{8,9},{9,8},{10,11... | collective-permute-start | bytes 6291464 | tf_op jit(solution)/shard_map/ppermute | solution.py:37
  258.6 89.4 %collective-permute-start.3 = (bf16[512,2048]{1,0:T(8,128)(2,1)S(1)}, bf16[512,2048]{1,0:T(8,128)(2,1)}, u32[]{:S(2)}, u32[]{:S(2)}) collective-permute-start(bf16[512,2048]{1,0:T(8,128)(2,1)S(1)} %copy-done.3), channel_id=1, source_target_pairs={{0,1},{1,0},{2,3},{3,2},{4,5},{5,4},{6,7},{7,6},{8,9},{9,8},{10,11... | collective-permute-start | bytes 6291464 | tf_op jit(solution)/shard_map/ppermute | solution.py:37
Sparse Core Ops, SparseCore 0:
  9.6 48.6 all-gather.10
  59.8 44.6 all-gather.6
  107.6 39.9 reduce-scatter.8
  150.8 41.2 reduce-scatter.4
  196.9 31.5 all-gather.8
  230.4 31.4 all-gather.12
  263.5 31.4 all-gather.14
  296.6 31.4 all-gather.16
  331.1 43.8 reduce-scatter.6
  377.8 43.1 reduce-scatter.10

commit v2 on v1

v2 whole, which is shorter than its diff:
```python
import functools

import jax
import jax.numpy as jnp
from jax import lax
from jax.experimental import pallas as pl
from jax.experimental.pallas import tpu as pltpu
from jax.sharding import PartitionSpec as P

LEVELS = 4
CORES = 2
CHUNKS = 2
VMEM_LIMIT = 56 << 20


sharpness = 4.0


def spike_parts(potential, gain):
    scaled = potential * gain[None, :]
    total = jnp.zeros_like(scaled)
    slope = jnp.zeros_like(scaled)
    for level in range(LEVELS):
        sig = jax.nn.sigmoid(sharpness * (scaled - (level + 0.5)))
        total = total + sig
        slope = slope + sig * (1.0 - sig)
    return (total, slope * (sharpness * gain[None, :]))


def wide(value):
    return value.astype(jnp.float32)


def narrow(value):
    return value.astype(jnp.bfloat16)


def tile_of(size, most):
    best = 128
    for tile in range(128, most + 1, 128):
        if size % tile == 0:
            best = tile
    return best


def product(left, right, contract):
    return lax.dot_general(
        left, right, (contract, ((), ())), preferred_element_type=jnp.float32
    )


HERE = pl.BlockSpec(memory_space=pl.ANY)
NO_COST = pl.CostEstimate(flops=0, bytes_accessed=0, transcendentals=0)
PARAMS = pltpu.CompilerParams(vmem_limit_bytes=VMEM_LIMIT)


def copy_all(pairs, sems):
    copies = [
        pltpu.make_async_copy(source, target, sems.at[i])
        for i, (source, target) in enumerate(pairs)
    ]
    for copy in copies:
        copy.start()
    for copy in copies:
        copy.wait()


def slot_places(slots, held):
    rows = slots[0].shape[0]
    return [(slot, held.at[pl.ds(i * rows, rows)]) for i, slot in enumerate(slots)]


def plain_rows(me, core, chip_away, rows, first):
    chip = jnp.bitwise_xor(lax.div(me, CORES), chip_away)
    return pl.ds(pl.multiple_of(first + (chip * CORES + core) * rows, rows), rows)


def gathered_places(me, rows, gathered, held):
    places, first = [], 0
    for value in gathered:
        for core in range(CORES):
            for k in range(value.shape[1] // rows):
                source = value.at[core, pl.ds(k * rows, rows)]
                places.append((source, held.at[plain_rows(me, core, k, rows, first)]))
        first += CORES * value.shape[1]
    return places


def far_places(me, chips, parts, held, first):
    places, rows = [], parts[0].shape[0]
    for i, part in enumerate(parts):
        chunk, at = divmod(i, CORES * chips)
        core = lax.rem(me + at // chips, CORES)
        start = first + chunk * CORES * chips * rows
        where = plain_rows(me, core, at % chips, rows, start)
        places.append((part, held.at[where]))
    return places


def weight_spec(weight, tile, transposed):
    if transposed:
        return pl.BlockSpec((tile, weight.shape[1]), lambda j, me: (j, 0))
    return pl.BlockSpec((weight.shape[0], tile), lambda j, me: (0, j))


def project_kernel(rows, contract, n_slots, me, *refs):
    slots, weight, out = refs[:n_slots], refs[n_slots], refs[n_slots + 1]
    held, sems = refs[-2:]

    @pl.when(pl.program_id(0) == 0)
    def _():
        height = slots[0].shape[0]
        chips = held.shape[0] // rows // CORES
        piece, places = min(rows, height), []
        for first in range(0, held.shape[0], piece):
            part, within = divmod(first, rows)
            away = jnp.bitwise_xor(lax.div(me[0], CORES), part // CORES)
            at = (part % CORES * chips + away) * rows + within
            source = slots[first // height].at[pl.ds(first % height, piece)]
            target = held.at[pl.ds(pl.multiple_of(at, piece), piece)]
            places.append((source, target))
        copy_all(places, sems)

    result = narrow(product(held[...], weight[...], contract))
    cut = result.shape[0] // CORES
    for core in range(CORES):
        out[core] = result[core * cut : (core + 1) * cut]


def project(me, rows, slots, weight, transposed):
    total = sum(s.shape[0] for s in slots)
    depth = slots[0].shape[1]
    width = weight.shape[0 if transposed else 1]
    tile = tile_of(width, 512)
    cut = total // CORES
    contract = ((1,), (1,)) if transposed else ((1,), (0,))
    return pl.pallas_call(
        functools.partial(project_kernel, rows, contract, len(slots)),
        grid_spec=pltpu.PrefetchScalarGridSpec(
            num_scalar_prefetch=1,
            grid=(width // tile,),
            in_specs=[HERE] * len(slots) + [weight_spec(weight, tile, transposed)],
            out_specs=pl.BlockSpec((CORES, cut, tile), lambda j, me: (0, 0, j)),
            scratch_shapes=[
                pltpu.VMEM((total, depth), jnp.bfloat16),
                pltpu.SemaphoreType.DMA((max(total // rows, len(slots)),)),
            ],
        ),
        out_shape=jax.ShapeDtypeStruct((CORES, cut, width), jnp.bfloat16),
        compiler_params=PARAMS,
        cost_estimate=NO_COST,
    )(me, *slots, weight)


def expand_kernel(rows, contract, me, gathered, weight, *refs):
    outs, held, sems = refs[:-2], refs[-2], refs[-1]

    @pl.when(pl.program_id(0) == 0)
    def _():
        copy_all(gathered_places(me[0], rows, [gathered], held), sems)

    result = narrow(product(held[...], weight[...], contract))
    each = outs[0].shape[0]
    for s, out in enumerate(outs):
        out[...] = result[s * each : (s + 1) * each]


def expand(me, rows, gathered, n_slots, weight, transposed):
    total = CORES * gathered.shape[1]
    depth = gathered.shape[2]
    width = weight.shape[0 if transposed else 1]
    tile = tile_of(width, 256)
    each = total // n_slots
    contract = ((1,), (1,)) if transposed else ((1,), (0,))
    return pl.pallas_call(
        functools.partial(expand_kernel, rows, contract),
        grid_spec=pltpu.PrefetchScalarGridSpec(
            num_scalar_prefetch=1,
            grid=(width // tile,),
            in_specs=[HERE, weight_spec(weight, tile, transposed)],
            out_specs=[pl.BlockSpec((each, tile), lambda j, me: (0, j))] * n_slots,
            scratch_shapes=[
                pltpu.VMEM((total, depth), jnp.bfloat16),
                pltpu.SemaphoreType.DMA((total // rows,)),
            ],
        ),
        out_shape=[jax.ShapeDtypeStruct((each, width), jnp.bfloat16)] * n_slots,
        compiler_params=PARAMS,
        cost_estimate=NO_COST,
    )(me, gathered, weight)


def weight_kernel(rows, chips, parts_left, counts, tile, me, *refs):
    n_slots, n_gathered, n_far = counts
    slots, gathered = refs[:n_slots], refs[n_slots : n_slots + n_gathered]
    far = refs[n_slots + n_gathered : n_slots + n_gathered + n_far]
    out, held_slots, held_parts, sems = refs[-4:]
    step = pl.program_id(0)

    @pl.when(step == 0)
    def _():
        places = slot_places(slots, held_slots)
        places += gathered_places(me[0], rows, gathered, held_parts)
        first = sum(CORES * value.shape[1] for value in gathered)
        places += far_places(me[0], chips, far, held_parts, first)
        copy_all(places, sems)

    left, right = (held_parts, held_slots) if parts_left else (held_slots, held_parts)
    columns = left[:, pl.ds(pl.multiple_of(step * tile, tile), tile)]
    out[...] = narrow(product(columns, right[...], ((0,), (0,))))


def weight_product(me, rows, chips, slots, gathered, far, parts_left):
    total = sum(s.shape[0] for s in slots)
    slot_width, part_width = slots[0].shape[1], far[0].shape[1]
    tall, width = (part_width, slot_width) if parts_left else (slot_width, part_width)
    tile = tile_of(tall, 256)
    counts = (len(slots), len(gathered), len(far))
    copies = len(slots) + len(gathered) * CORES * chips + len(far)
    return pl.pallas_call(
        functools.partial(weight_kernel, rows, chips, parts_left, counts, tile),
        grid_spec=pltpu.PrefetchScalarGridSpec(
            num_scalar_prefetch=1,
            grid=(tall // tile,),
            in_specs=[HERE] * sum(counts),
            out_specs=pl.BlockSpec((tile, width), lambda j, me: (j, 0)),
            scratch_shapes=[
                pltpu.VMEM((total, slot_width), jnp.bfloat16),
                pltpu.VMEM((total, part_width), jnp.bfloat16),
                pltpu.SemaphoreType.DMA((copies,)),
            ],
        ),
        out_shape=jax.ShapeDtypeStruct((tall, width), jnp.bfloat16),
        compiler_params=PARAMS,
        cost_estimate=NO_COST,
    )(me, *slots, *gathered, *far)


class Program:
    def __init__(self, token):
        self.token = token

    def placed(self, values):
        return lax.optimization_barrier((*values, self.token))[:-1]

    def passed(self, values):
        *values, self.token = lax.optimization_barrier((*values, self.token))
        return values

    def start(self, value, axis, pairs):
        (value,) = self.placed([value])
        return lax.ppermute(value, axis, pairs)

    def wait(self, moving):
        return self.passed([moving])[0]

    def compute(self, step, *values):
        done = step(*self.placed(values))
        if isinstance(done, (tuple, list)):
            return self.passed(done)
        return self.passed([done])[0]


def shards(sizes, tokens, w_in, w_out, spike_gain, cotangent):
    n_row, n_col, n_dp = sizes["row"], sizes["col"], sizes["dp"]
    chips = n_col // CORES
    chunks = CHUNKS if n_row % CHUNKS == 0 else 1
    per = n_row // chunks
    part = per * tokens.shape[0] // n_col
    me = lax.axis_index("col").astype(jnp.int32).reshape(1)
    run = Program(me)

    def row_start(value):
        return run.start(value, "row", [(i, (i + 1) % n_row) for i in range(n_row)])

    def core_start(value):
        return run.start(value, "col", [(i, i ^ 1) for i in range(n_col)])

    def cores_exchange(value):
        pairs = [list(range(i, i + CORES)) for i in range(0, n_col, CORES)]
        return lax.all_to_all(value, "col", 0, 0, axis_index_groups=pairs)

    def chip_start(values):
        return [
            run.start(value, "col", [(i, i ^ (CORES * k)) for i in range(n_col)])
            for k, value in zip(range(1, chips), values)
        ]

    def half_start(value):
        return [
            run.start(value, "dp", [(d, (d + k) % n_dp) for d in range(n_dp)])
            for k in range(1, n_dp)
        ]

    def wait_all(moving):
        return [run.wait(value) for value in moving]

    def forward(*slots):
        return project(me, part, slots, w_in, False)

    def backward(*slots):
        return project(me, part, slots, w_out, True)

    def expand_out(gathered):
        return expand(me, part, gathered, per, w_out, False)

    def expand_back(gathered):
        return expand(me, part, gathered, per, w_in, True)

    def part_sum(partial, k):
        rows = slice(k * part, (k + 1) * part)
        return sum(wide(partial[core, rows]) for core in range(CORES))

    def chip_sums(partial):
        return [narrow(part_sum(partial, k)) for k in range(1, chips)]

    def whole(partial, arrived):
        total = part_sum(partial, 0)
        for value in arrived:
            total = total + wide(value)
        return total

    def fire(partial, *arrived):
        total, slope = spike_parts(whole(partial, arrived), spike_gain)
        return narrow(total), slope

    def slope_back(partial, slope, *arrived):
        return narrow(whole(partial, arrived) * slope)

    def both_cores(*held):
        mine = jnp.concatenate(held, axis=0)
        return cores_exchange(jnp.stack([mine] * CORES))

    def ring_add(arrived, slot):
        return narrow(wide(arrived) + wide(slot))

    def weight_step(parts_left):
        def weights(*values):
            slots, gathered = values[:n_all], values[n_all : n_all + chunks]
            far_parts = values[n_all + chunks :]
            return weight_product(me, part, chips, slots, gathered, far_parts, parts_left)

        return weights

    n_all = n_row * n_dp
    tok, cot, outs, back, summed = [], [], [], [], []

    def row_lane():
        for own, slots in ((tokens, tok), (cotangent, cot)):
            slots.append(own)
            for _ in range(n_row - 1):
                moving = row_start(slots[-1])
                yield
                slots.append(run.wait(moving))
        for slots in (outs, back):
            held = slots[1 % n_row]
            for s in range(2, n_row + 1):
                moving = row_start(held)
                yield
                held = run.compute(ring_add, run.wait(moving), slots[s % n_row])
            summed.append(held)

    row = row_lane()

    def turn():
        next(row, None)

    def until(slots, count):
        while len(slots) < count:
            turn()

    first, second = list(range(per)), list(range(per, n_row))
    far = {}
    spikes, slopes, grads = [], [], []
    sources = {"tok": tok, "cot": cot, "spike": spikes, "grad": grads}

    def half_lane():
        queue = [("tok", s) for s in first]
        queue += [("spike", 0)] + [("tok", s) for s in second[:1]]
        queue += [("spike", c) for c in range(1, chunks)]
        queue += [("tok", s) for s in second[1:]]
        queue += [("grad", 0), ("cot", 0)] + [("grad", c) for c in range(1, chunks)]
        queue += [("cot", s) for s in range(1, n_row)]
        for kind, at in queue:
            moving = half_start(sources[kind][at])
            yield
            far[kind, at] = wait_all(moving)

    half = half_lane()

    def half_turn():
        next(half, None)

    def projected(step, slots):
        return run.compute(cores_exchange, run.compute(step, *slots))

    def spreading(value):
        return value, chip_start([value] * (chips - 1))

    def chunk(slots, c):
        return slots[c * per : (c + 1) * per]

    turn()
    half_turn()
    until(tok, per)
    partial = projected(forward, chunk(tok, 0))
    moving = chip_start(run.compute(chip_sums, partial))
    half_turn()
    until(tok, n_row - 1)
    spike, slope = run.compute(fire, partial, *wait_all(moving))
    spikes.append(spike)
    slopes.append(slope)
    gather = spreading(spike)
    half_turn()
    until(tok, n_row)

    grad_partials, grad_sums, spike_all = [], [], []

    def project_back(c):
        until(cot, (c + 1) * per)
        grad_partials.append(projected(backward, chunk(cot, c)))
        grad_sums.append(run.compute(chip_sums, grad_partials[c]))

    def gathered(value, moving):
        return run.compute(both_cores, value, *wait_all(moving))

    for c in range(1, chunks):
        partial = projected(forward, chunk(tok, c))
        sums = run.compute(chip_sums, partial)
        arrived = wait_all(gather[1])
        moving = chip_start(sums)
        spike_all.append(run.compute(both_cores, gather[0], *arrived))
        half_turn()
        if c == 1:
            project_back(0)
        spike, slope = run.compute(fire, partial, *wait_all(moving))
        spikes.append(spike)
        slopes.append(slope)
        gather = spreading(spike)
        half_turn()
        outs.extend(run.compute(expand_out, spike_all[c - 1]))
    if chunks == 1:
        project_back(0)
    until(cot, n_row - 1)
    arrived = wait_all(gather[1])
    grad_moving = chip_start(grad_sums[0])
    half_turn()
    spike_all.append(run.compute(both_cores, gather[0], *arrived))
    outs.extend(run.compute(expand_out, spike_all[chunks - 1]))
    until(cot, n_row)

    grad_all = []
    for c in range(chunks):
        grad = run.compute(
            slope_back, grad_partials[c], slopes[c], *wait_all(grad_moving)
        )
        grads.append(grad)
        gather = spreading(grad)
        half_turn()
        if c + 1 < chunks:
            project_back(c + 1)
        else:
            turn()
        arrived = wait_all(gather[1])
        if c + 1 < chunks:
            grad_moving = chip_start(grad_sums[c + 1])
            turn()
        else:
            far_moving = chip_start(far["spike", 0][:1] * (chips - 1))
        half_turn()
        grad_all.append(run.compute(both_cores, gather[0], *arrived))
        back.extend(run.compute(expand_back, grad_all[c]))
    turn()

    todo = [
        (kind, c, h)
        for kind in ("spike", "grad")
        for h in range(n_dp - 1)
        for c in range(chunks)
    ]
    spread = {"spike": [], "grad": []}
    waiting = None

    def settle():
        if waiting is not None:
            kind, held, others = waiting
            spread[kind].extend(held + wait_all(others))

    def every(kind, slots):
        return slots + [far[kind, s][h] for h in range(n_dp - 1) for s in range(n_row)]

    for i, (kind, c, h) in enumerate(todo):
        own = far[kind, c][h]
        arrived = wait_all(far_moving)
        beside = [core_start(value) for value in [own] + arrived]
        if i + 1 < len(todo):
            kind_next, c_next, h_next = todo[i + 1]
            while (kind_next, c_next) not in far:
                half_turn()
            far_moving = chip_start([far[kind_next, c_next][h_next]] * (chips - 1))
        half_turn()
        settle()
        waiting = (kind, [own] + arrived, beside)
        if i + 2 == len(todo):
            while ("cot", n_row - 1) not in far:
                half_turn()
            weight_out = run.compute(
                weight_step(True), *every("cot", cot), *spike_all, *spread["spike"]
            )
        turn()
    settle()
    while len(summed) < 2:
        turn()
    weight_in = run.compute(
        weight_step(False), *every("tok", tok), *grad_all, *spread["grad"]
    )
    return (summed[0], summed[1], weight_in, weight_out)


def solution(mesh):
    placed = (
        P(("dp", "row"), "col"),
        P("col", "row"),
        P("row", "col"),
        P("row"),
        P(("dp", "row"), "col"),
    )

    def program(*args):
        return shards(mesh.shape, *args)

    return jax.shard_map(
        program,
        mesh=mesh,
        in_specs=placed,
        out_specs=(
            P(("dp", "row"), "col"),
            P(("dp", "row"), "col"),
            P("col", "row"),
            P("row", "col"),
        ),
        check_vma=False,
    )
```

time: 428 us -> 327 us (0.76)
  waiting for transfers between devices: 305 us -> 77.2 us
  Pallas kernels: 0 us -> 142 us
  matrix products: 95.9 us -> 0 us
  blocking collectives: 0 us -> 50.1 us
  starting transfers between devices: 5.75 us -> 41.8 us
  between operations: 14.2 us -> 1.51 us
  other arithmetic: 4.71 us -> 9.66 us
    pallas_call x0 -> x10, Pallas kernels: none -> 142 us  [the longest x4 48.5 us: expand(): pl.pallas_call(functools.partial(expand_kernel, rows, contract), grid_spe...]
    reduce_scatter x4 -> x0, waiting for transfers between devices: 125 us -> none  [scattered(): lax.psum_scatter(value.astype(jnp.bfloat16), axis, scatter_dimension=0, t...]
    dot_general x6 -> x0, matrix products: 95.9 us -> none  [the longest x2 43.7 us: over_tokens(): lax.dot_general(left, right, (((0,), (0,)), ((), ())), preferred_element_...]
    all_gather x6 -> x0, waiting for transfers between devices: 85.7 us -> none  [gathered(): return lax.all_gather(value, axis, axis=0, tiled=True)]
    all_to_all x0 -> x8, blocking collectives: none -> 50.1 us  [cores_exchange(): return lax.all_to_all(value, 'col', 0, 0, axis_index_groups=pairs)]
    ppermute x4 -> x44, starting transfers between devices: 5.17 us -> 41.8 us  [start(): return lax.ppermute(value, axis, pairs)]
    ppermute x4 -> x44, waiting for transfers between devices: 91.6 us -> 77.2 us  [start(): return lax.ppermute(value, axis, pairs)]
  transfers between devices with their start and end apart: 14 -> 44, of which waited for: 11 -> 12; matrix products, arithmetic and copies ran while one was open for 22% -> 3% of each run, Pallas kernels for 0% -> 37%
where the time goes in v2:
time: 327 us; the launch traced here: 326 us
  Pallas kernels  142 us (43%)
  waiting for transfers between devices  77.2 us (24%)
  blocking collectives  50.1 us (15%)
  starting transfers between devices  41.8 us (13%)
  other arithmetic  9.66 us (3%)
  local copies, waits for them, and re-layouts  3.4 us (1%)
    ppermute x44, waiting for transfers between devices, start(): return lax.ppermute(value, axis, pairs)  77.2 us
    all_to_all x8, blocking collectives, cores_exchange(): return lax.all_to_all(value, 'col', 0, 0, axis_index_groups=pairs)  50.1 us
    pallas_call x4, Pallas kernels, expand(): pl.pallas_call(functools.partial(expand_kernel, rows, contract), grid_spe...  48.5 us
    pallas_call x4, Pallas kernels, project(): pl.pallas_call(functools.partial(project_kernel, rows, contract, len(slot...  47.1 us
    pallas_call x2, Pallas kernels, weight_product(): pl.pallas_call(functools.partial(weight_kernel, rows, chips, parts_left,...  46.5 us
    ppermute x44, starting transfers between devices, start(): return lax.ppermute(value, axis, pairs)  41.8 us
  transfers between devices with their start and end apart: 44, of which 12 were waited for; matrix products, arithmetic and copies ran while one was open for 3% of the time, Pallas kernels for 37%

profile of v2, /device:TPU:0, one launch (start us, length us, event | category | flops | bytes accessed | tf_op | source)
XLA Modules:
  0.0 325.7 jit_solution(18050737895129113366)
XLA Ops:
  0.6 3.1 collective-permute-start
  5.2 12.7 %collective-permute-done.refs_1_ = bf16[128,2048]{1,0:T(8,128)(2,1)} collective-permute-done((bf16[128,2048]{1,0:T(8,128)(2,1)}, bf16[128,2048]{1,0:T(8,128)(2,1)}, u32[]{:S(2)}, u32[]{:S(2)}) %collective-permute-start) | collective-permute-done | bytes 524320 | tf_op jit(solution)/shard_map/ppermute | solution.py:252
  18.0 11.7 %shard_map.84 = bf16[2,128,3584]{2,1,0:T(8,128)(2,1)} custom-call(s32[1]{0:T(128)} %bitcast.me, bf16[128,2048]{1,0:T(8,128)(2,1)} %refs_0_.3, bf16[128,2048]{1,0:T(8,128)(2,1)} %collective-permute-done.refs_1_, bf16[2048,3584]{1,0:T(8,128)(2,1)} %weight.7), custom_call_target="tpu_custom_call" | custom-call | tf_op jit(solution)/shard_map/pallas_call | solution.py:137
  29.7 6.4 %all_to_all.40 = bf16[2,128,3584]{2,1,0:T(8,128)(2,1)S(1)} all-to-all(bf16[2,128,3584]{2,1,0:T(8,128)(2,1)} %shard_map.84), channel_id=1, replica_groups={{0,2},{4,6},{1,3},{5,7},{8,10},{12,14},{9,11},{13,15},{16,18},{20,22},{..., dimensions={0} | all-to-all | bytes 3670016 | tf_op jit(solution)/shard_map/all_to_all | solution.py:281
  37.8 1.6 collective-permute-start.6
  39.4 9.5 %collective-permute-done.1 = bf16[64,3584]{1,0:T(8,128)(2,1)S(1)} collective-permute-done((bf16[64,3584]{1,0:T(8,128)(2,1)S(1)}, bf16[64,3584]{1,0:T(8,128)(2,1)S(1)}, u32[]{:S(2)}, u32[]{:S(2)}) %collective-permute-start.1) | collective-permute-done | bytes 458784 | tf_op jit(solution)/shard_map/ppermute | solution.py:252
  54.6 9.5 %collective-permute-done.5.refs_1_.refs_3_ = bf16[128,2048]{1,0:T(8,128)(2,1)S(1)} collective-permute-done((bf16[128,2048]{1,0:T(8,128)(2,1)S(1)}, bf16[128,2048]{1,0:T(8,128)(2,1)S(1)}, u32[]{:S(2)}, u32[]{:S(2)}) %collective-permute-start.5) | collective-permute-done | bytes 524320 | tf_op jit(solution)/shard_map/ppermute | solution.py:252
  64.8 11.7 %shard_map.85 = bf16[2,128,3584]{2,1,0:T(8,128)(2,1)} custom-call(s32[1]{0:T(128)} %bitcast.me, bf16[128,2048]{1,0:T(8,128)(2,1)} %copy-done.2, bf16[128,2048]{1,0:T(8,128)(2,1)} %copy-done.4, bf16[2048,3584]{1,0:T(8,128)(2,1)} %weight.7), custom_call_target="tpu_custom_call" | custom-call | tf_op jit(solution)/shard_map/pallas_call | solution.py:137
  76.6 6.4 %all_to_all.41 = bf16[2,128,3584]{2,1,0:T(8,128)(2,1)S(1)} all-to-all(bf16[2,128,3584]{2,1,0:T(8,128)(2,1)} %shard_map.85), channel_id=1, replica_groups={{0,2},{4,6},{1,3},{5,7},{8,10},{12,14},{9,11},{13,15},{16,18},{20,22},{..., dimensions={0} | all-to-all | bytes 3670016 | tf_op jit(solution)/shard_map/all_to_all | solution.py:281
  84.9 6.2 %all_to_all.42.gathered.refs_8_ = bf16[2,128,3584]{2,1,0:T(8,128)(2,1)} all-to-all(bf16[2,128,3584]{2,1,0:T(8,128)(2,1)S(1)} %pad_maximum_fusion), channel_id=1, replica_groups={{0,2},{4,6},{1,3},{5,7},{8,10},{12,14},{9,11},{13,15},{16,18},{20,22},{..., dimensions={0} | all-to-all | bytes 3670016 | tf_op jit(solution)/shard_map/all_to_all | solution.py:281
  91.1 1.6 collective-permute-start.8
  93.5 11.8 %shard_map.86 = bf16[2,128,3584]{2,1,0:T(8,128)(2,1)} custom-call(s32[1]{0:T(128)} %bitcast.me, bf16[128,2048]{1,0:T(8,128)(2,1)} %refs_0_.2, bf16[128,2048]{1,0:T(8,128)(2,1)} %copy-done.6, bf16[3584,2048]{1,0:T(8,128)(2,1)} %refs_2_.7), custom_call_target="tpu_custom_call" | custom-call | tf_op jit(solution)/shard_map/pallas_call | solution.py:137
  105.4 6.4 %all_to_all.43 = bf16[2,128,3584]{2,1,0:T(8,128)(2,1)S(1)} all-to-all(bf16[2,128,3584]{2,1,0:T(8,128)(2,1)} %shard_map.86), channel_id=1, replica_groups={{0,2},{4,6},{1,3},{5,7},{8,10},{12,14},{9,11},{13,15},{16,18},{20,22},{..., dimensions={0} | all-to-all | bytes 3670016 | tf_op jit(solution)/shard_map/all_to_all | solution.py:281
  112.6 2.4 fusion.7
  116.2 12.0 %shard_map.87 = (bf16[128,2048]{1,0:T(8,128)(2,1)}, bf16[128,2048]{1,0:T(8,128)(2,1)}) custom-call(s32[1]{0:T(128)} %bitcast.me, bf16[2,128,3584]{2,1,0:T(8,128)(2,1)} %all_to_all.42.gathered.refs_8_, bf16[3584,2048]{1,0:T(8,128)(2,1)} %refs_2_.7), custom_call_target="tpu_custom_call" | custom-call | tf_op jit(solution)/shard_map/pallas_call | solution.py:175
  132.8 6.1 %all_to_all.44.gathered.refs_9_ = bf16[2,128,3584]{2,1,0:T(8,128)(2,1)} all-to-all(bf16[2,128,3584]{2,1,0:T(8,128)(2,1)S(1)} %pad_maximum_fusion.1), channel_id=1, replica_groups={{0,2},{4,6},{1,3},{5,7},{8,10},{12,14},{9,11},{13,15},{16,18},{20,22},{..., dimensions={0} | all-to-all | bytes 3670016 | tf_op jit(solution)/shard_map/all_to_all | solution.py:281
  138.9 12.0 %shard_map.88 = (bf16[128,2048]{1,0:T(8,128)(2,1)}, bf16[128,2048]{1,0:T(8,128)(2,1)}) custom-call(s32[1]{0:T(128)} %bitcast.me, bf16[2,128,3584]{2,1,0:T(8,128)(2,1)} %all_to_all.44.gathered.refs_9_, bf16[3584,2048]{1,0:T(8,128)(2,1)} %refs_2_.7), custom_call_target="tpu_custom_call" | custom-call | tf_op jit(solution)/shard_map/pallas_call | solution.py:175
  152.5 2.1 collective-permute-start.15
  154.6 11.8 %shard_map.89 = bf16[2,128,3584]{2,1,0:T(8,128)(2,1)} custom-call(s32[1]{0:T(128)} %bitcast.me, bf16[128,2048]{1,0:T(8,128)(2,1)} %copy-done.8, bf16[128,2048]{1,0:T(8,128)(2,1)} %copy-done.10, bf16[3584,2048]{1,0:T(8,128)(2,1)} %refs_2_.7), custom_call_target="tpu_custom_call" | custom-call | tf_op jit(solution)/shard_map/pallas_call | solution.py:137
  166.4 6.5 %all_to_all.45 = bf16[2,128,3584]{2,1,0:T(8,128)(2,1)S(1)} all-to-all(bf16[2,128,3584]{2,1,0:T(8,128)(2,1)} %shard_map.89), channel_id=1, replica_groups={{0,2},{4,6},{1,3},{5,7},{8,10},{12,14},{9,11},{13,15},{16,18},{20,22},{..., dimensions={0} | all-to-all | bytes 3670016 | tf_op jit(solution)/shard_map/all_to_all | solution.py:281
  177.2 6.1 %all_to_all.46.gathered.refs_8_ = bf16[2,128,3584]{2,1,0:T(8,128)(2,1)} all-to-all(bf16[2,128,3584]{2,1,0:T(8,128)(2,1)S(1)} %pad_maximum_fusion.2), channel_id=1, replica_groups={{0,2},{4,6},{1,3},{5,7},{8,10},{12,14},{9,11},{13,15},{16,18},{20,22},{..., dimensions={0} | all-to-all | bytes 3670016 | tf_op jit(solution)/shard_map/all_to_all | solution.py:281
  183.3 12.1 %shard_map.90 = (bf16[128,2048]{1,0:T(8,128)(2,1)}, bf16[128,2048]{1,0:T(8,128)(2,1)}) custom-call(s32[1]{0:T(128)} %bitcast.me, bf16[2,128,3584]{2,1,0:T(8,128)(2,1)} %all_to_all.46.gathered.refs_8_, bf16[2048,3584]{1,0:T(8,128)(2,1)} %weight.7), custom_call_target="tpu_custom_call" | custom-call | tf_op jit(solution)/shard_map/pallas_call | solution.py:175
  199.2 10.2 %collective-permute-done.24 = bf16[64,3584]{1,0:T(8,128)(2,1)S(1)} collective-permute-done((bf16[64,3584]{1,0:T(8,128)(2,1)S(1)}, bf16[64,3584]{1,0:T(8,128)(2,1)S(1)}, u32[]{:S(2)}, u32[]{:S(2)}) %collective-permute-start.24) | collective-permute-done | bytes 458784 | tf_op jit(solution)/shard_map/ppermute | solution.py:252
  210.7 6.1 %all_to_all.47.gathered.refs_9_ = bf16[2,128,3584]{2,1,0:T(8,128)(2,1)} all-to-all(bf16[2,128,3584]{2,1,0:T(8,128)(2,1)S(1)} %pad_maximum_fusion.3), channel_id=1, replica_groups={{0,2},{4,6},{1,3},{5,7},{8,10},{12,14},{9,11},{13,15},{16,18},{20,22},{..., dimensions={0} | all-to-all | bytes 3670016 | tf_op jit(solution)/shard_map/all_to_all | solution.py:281
  216.8 12.3 %shard_map.91 = (bf16[128,2048]{1,0:T(8,128)(2,1)}, bf16[128,2048]{1,0:T(8,128)(2,1)}) custom-call(s32[1]{0:T(128)} %bitcast.me, bf16[2,128,3584]{2,1,0:T(8,128)(2,1)} %all_to_all.47.gathered.refs_9_, bf16[2048,3584]{1,0:T(8,128)(2,1)} %weight.7), custom_call_target="tpu_custom_call" | custom-call | tf_op jit(solution)/shard_map/pallas_call | solution.py:175
  232.2 11.1 %collective-permute-done.28.refs_11_ = bf16[64,3584]{1,0:T(8,128)(2,1)S(1)} collective-permute-done((bf16[64,3584]{1,0:T(8,128)(2,1)S(1)}, bf16[64,3584]{1,0:T(8,128)(2,1)S(1)}, u32[]{:S(2)}, u32[]{:S(2)}) %collective-permute-start.28) | collective-permute-done | bytes 458784 | tf_op jit(solution)/shard_map/ppermute | solution.py:252
  243.3 1.6 collective-permute-start.32
  248.1 9.9 %collective-permute-done.33.refs_15_ = bf16[64,3584]{1,0:T(8,128)(2,1)S(1)} collective-permute-done((bf16[64,3584]{1,0:T(8,128)(2,1)S(1)}, bf16[64,3584]{1,0:T(8,128)(2,1)S(1)}, u32[]{:S(2)}, u32[]{:S(2)}) %collective-permute-start.33) | collective-permute-done | bytes 458784 | tf_op jit(solution)/shard_map/ppermute | solution.py:252
  258.1 1.6 collective-permute-start.35
  263.2 9.1 %collective-permute-done.36.refs_11_ = bf16[64,3584]{1,0:T(8,128)(2,1)S(1)} collective-permute-done((bf16[64,3584]{1,0:T(8,128)(2,1)S(1)}, bf16[64,3584]{1,0:T(8,128)(2,1)S(1)}, u32[]{:S(2)}, u32[]{:S(2)}) %collective-permute-start.36) | collective-permute-done | bytes 458784 | tf_op jit(solution)/shard_map/ppermute | solution.py:252
  274.6 23.8 %shard_map.92 = bf16[3584,2048]{1,0:T(8,128)(2,1)} custom-call(s32[1]{0:T(128)} %bitcast.me, bf16[128,2048]{1,0:T(8,128)(2,1)} %refs_0_.2, bf16[128,2048]{1,0:T(8,128)(2,1)} %copy-done.6, bf16[128,2048]{1,0:T(8,128)(2,1)} %copy-done.8, bf16[128,2048]{1,0:T(8,128)(2,1)} %copy-done.10, bf16[128,2048]{1,0:T(8,128)(2,1)} %copy-done.16, ...), custom_call_target="tpu_custom_call" | custom-call | tf_op jit(solution)/shard_map/pallas_call | solution.py:220
  302.8 22.7 %shard_map.93 = bf16[2048,3584]{1,0:T(8,128)(2,1)} custom-call(s32[1]{0:T(128)} %bitcast.me, bf16[128,2048]{1,0:T(8,128)(2,1)} %refs_0_.3, bf16[128,2048]{1,0:T(8,128)(2,1)} %collective-permute-done.refs_1_, bf16[128,2048]{1,0:T(8,128)(2,1)} %copy-done.2, bf16[128,2048]{1,0:T(8,128)(2,1)} %copy-done.4, bf16[128,2048]{1,0:T(8,128)(2,1)} %copy-done.12, ...), custom_call_target="tpu_custom_call" | custom-call | tf_op jit(solution)/shard_map/pallas_call | solution.py:220
  (187 shorter events, 46.1 us)
Async XLA Ops:
  0.6 17.3 %collective-permute-start = (bf16[128,2048]{1,0:T(8,128)(2,1)}, bf16[128,2048]{1,0:T(8,128)(2,1)}, u32[]{:S(2)}, u32[]{:S(2)}) collective-permute-start(bf16[128,2048]{1,0:T(8,128)(2,1)} %refs_0_.3), channel_id=1, source_target_pairs={{0,8},{8,16},{16,24},{24,0},{1,9},{9,17},{17,25},{25,1},{2,10},{10... | collective-permute-start | bytes 1572872 | tf_op jit(solution)/shard_map/ppermute | solution.py:252
  3.7 34.1 %collective-permute-start.3 = (bf16[128,2048]{1,0:T(8,128)(2,1)}, bf16[128,2048]{1,0:T(8,128)(2,1)S(1)}, u32[]{:S(2)}, u32[]{:S(2)}) collective-permute-start(bf16[128,2048]{1,0:T(8,128)(2,1)} %refs_0_.3), channel_id=1, source_target_pairs={{0,1},{1,0},{2,3},{3,2},{4,5},{5,4},{6,7},{7,6},{8,9},{9,8},{10,11... | collective-permute-start | bytes 1572872 | tf_op jit(solution)/shard_map/ppermute | solution.py:252
  18.0 21.4 %collective-permute-start.2 = (bf16[128,2048]{1,0:T(8,128)(2,1)}, bf16[128,2048]{1,0:T(8,128)(2,1)S(1)}, u32[]{:S(2)}, u32[]{:S(2)}) collective-permute-start(bf16[128,2048]{1,0:T(8,128)(2,1)} %collective-permute-done.refs_1_), channel_id=1, source_target_pairs={{0,8},{8,16},{16,24},{24,0},{1,9},{9,17},{17,25},{25,1},{2,10},{10... | collective-permute-start | bytes 1572872 | tf_op jit(solution)/shard_map/ppermute | solution.py:252
  36.2 12.6 %collective-permute-start.1 = (bf16[64,3584]{1,0:T(8,128)(2,1)S(1)}, bf16[64,3584]{1,0:T(8,128)(2,1)S(1)}, u32[]{:S(2)}, u32[]{:S(2)}) collective-permute-start(bf16[64,3584]{1,0:T(8,128)(2,1)S(1)} %fusion.14), channel_id=1, source_target_pairs={{0,4},{2,6},{4,0},{6,2},{1,5},{3,7},{5,1},{7,3},{8,12},{10,14},{12... | collective-permute-start | bytes 1376264 | tf_op jit(solution)/shard_map/ppermute | solution.py:252
  37.8 15.2 %collective-permute-start.6 = (bf16[128,2048]{1,0:T(8,128)(2,1)}, bf16[128,2048]{1,0:T(8,128)(2,1)S(1)}, u32[]{:S(2)}, u32[]{:S(2)}) collective-permute-start(bf16[128,2048]{1,0:T(8,128)(2,1)} %collective-permute-done.refs_1_), channel_id=1, source_target_pairs={{0,1},{1,0},{2,3},{3,2},{4,5},{5,4},{6,7},{7,6},{8,9},{9,8},{10,11... | collective-permute-start | bytes 1572872 | tf_op jit(solution)/shard_map/ppermute | solution.py:252
  48.8 15.2 %collective-permute-start.5 = (bf16[128,2048]{1,0:T(8,128)(2,1)S(1)}, bf16[128,2048]{1,0:T(8,128)(2,1)S(1)}, u32[]{:S(2)}, u32[]{:S(2)}) collective-permute-start(bf16[128,2048]{1,0:T(8,128)(2,1)S(1)} %collective-permute-done.2.refs_0_.refs_2_), channel_id=1, source_target_pairs={{0,8},{8,16},{16,24},{24,0},{1,9},{9,17},{17,25},{25,1},{2,10},{10... | collective-permute-start | bytes 1572872 | tf_op jit(solution)/shard_map/ppermute | solution.py:252
  51.5 31.6 %collective-permute-start.4 = (bf16[64,3584]{1,0:T(8,128)(2,1)S(1)}, bf16[64,3584]{1,0:T(8,128)(2,1)S(1)}, u32[]{:S(2)}, u32[]{:S(2)}) collective-permute-start(bf16[64,3584]{1,0:T(8,128)(2,1)S(1)} %get-tuple-element.335), channel_id=1, source_target_pairs={{0,4},{2,6},{4,0},{6,2},{1,5},{3,7},{5,1},{7,3},{8,12},{10,14},{12... | collective-permute-start | bytes 1376264 | tf_op jit(solution)/shard_map/ppermute | solution.py:252
  53.0 38.1 %collective-permute-start.7 = (bf16[64,3584]{1,0:T(8,128)(2,1)S(1)}, bf16[64,3584]{1,0:T(8,128)(2,1)S(1)}, u32[]{:S(2)}, u32[]{:S(2)}) collective-permute-start(bf16[64,3584]{1,0:T(8,128)(2,1)S(1)} %get-tuple-element.335), channel_id=1, source_target_pairs={{0,1},{1,0},{2,3},{3,2},{4,5},{5,4},{6,7},{7,6},{8,9},{9,8},{10,11... | collective-permute-start | bytes 1376264 | tf_op jit(solution)/shard_map/ppermute | solution.py:252
  64.1 28.7 %collective-permute-start.10 = (bf16[128,2048]{1,0:T(8,128)(2,1)S(1)}, bf16[128,2048]{1,0:T(8,128)(2,1)S(1)}, u32[]{:S(2)}, u32[]{:S(2)}) collective-permute-start(bf16[128,2048]{1,0:T(8,128)(2,1)S(1)} %copy-done), channel_id=1, source_target_pairs={{0,8},{8,16},{16,24},{24,0},{1,9},{9,17},{17,25},{25,1},{2,10},{10... | collective-permute-start | bytes 1572872 | tf_op jit(solution)/shard_map/ppermute | solution.py:252
  83.1 29.6 %collective-permute-start.9 = (bf16[64,3584]{1,0:T(8,128)(2,1)S(1)}, bf16[64,3584]{1,0:T(8,128)(2,1)}, u32[]{:S(2)}, u32[]{:S(2)}) collective-permute-start(bf16[64,3584]{1,0:T(8,128)(2,1)S(1)} %fusion.15), channel_id=1, source_target_pairs={{0,4},{2,6},{4,0},{6,2},{1,5},{3,7},{5,1},{7,3},{8,12},{10,14},{12... | collective-permute-start | bytes 1376264 | tf_op jit(solution)/shard_map/ppermute | solution.py:252
  91.1 24.5 %collective-permute-start.8 = (bf16[128,2048]{1,0:T(8,128)(2,1)S(1)}, bf16[128,2048]{1,0:T(8,128)(2,1)}, u32[]{:S(2)}, u32[]{:S(2)}) collective-permute-start(bf16[128,2048]{1,0:T(8,128)(2,1)S(1)} %copy-done.3), channel_id=1, source_target_pairs={{0,1},{1,0},{2,3},{3,2},{4,5},{5,4},{6,7},{7,6},{8,9},{9,8},{10,11... | collective-permute-start | bytes 1572872 | tf_op jit(solution)/shard_map/ppermute | solution.py:252
  92.7 35.5 %collective-permute-start.11 = (bf16[128,2048]{1,0:T(8,128)(2,1)S(1)}, bf16[128,2048]{1,0:T(8,128)(2,1)S(1)}, u32[]{:S(2)}, u32[]{:S(2)}) collective-permute-start(bf16[128,2048]{1,0:T(8,128)(2,1)S(1)} %collective-permute-done.10.refs_1_), channel_id=1, source_target_pairs={{0,8},{8,16},{16,24},{24,0},{1,9},{9,17},{17,25},{25,1},{2,10},{10... | collective-permute-start | bytes 1572872 | tf_op jit(solution)/shard_map/ppermute | solution.py:252
  115.0 13.1 %collective-permute-start.13 = (bf16[64,3584]{1,0:T(8,128)(2,1)S(1)}, bf16[64,3584]{1,0:T(8,128)(2,1)S(1)}, u32[]{:S(2)}, u32[]{:S(2)}) collective-permute-start(bf16[64,3584]{1,0:T(8,128)(2,1)S(1)} %get-tuple-element.370), channel_id=1, source_target_pairs={{0,4},{2,6},{4,0},{6,2},{1,5},{3,7},{5,1},{7,3},{8,12},{10,14},{12... | collective-permute-start | bytes 1376264 | tf_op jit(solution)/shard_map/ppermute | solution.py:252
  128.2 22.7 %collective-permute-start.16 = (bf16[64,3584]{1,0:T(8,128)(2,1)S(1)}, bf16[64,3584]{1,0:T(8,128)(2,1)S(1)}, u32[]{:S(2)}, u32[]{:S(2)}) collective-permute-start(bf16[64,3584]{1,0:T(8,128)(2,1)S(1)} %copy-done.39), channel_id=1, source_target_pairs={{0,4},{2,6},{4,0},{6,2},{1,5},{3,7},{5,1},{7,3},{8,12},{10,14},{12... | collective-permute-start | bytes 1376264 | tf_op jit(solution)/shard_map/ppermute | solution.py:252
  129.8 21.3 %collective-permute-start.18 = (bf16[128,2048]{1,0:T(8,128)(2,1)S(1)}, bf16[128,2048]{1,0:T(8,128)(2,1)S(1)}, u32[]{:S(2)}, u32[]{:S(2)}) collective-permute-start(bf16[128,2048]{1,0:T(8,128)(2,1)S(1)} %copy-done.5), channel_id=1, source_target_pairs={{0,1},{1,0},{2,3},{3,2},{4,5},{5,4},{6,7},{7,6},{8,9},{9,8},{10,11... | collective-permute-start | bytes 1572872 | tf_op jit(solution)/shard_map/ppermute | solution.py:252
  131.3 19.6 %collective-permute-start.12 = (bf16[128,2048]{1,0:T(8,128)(2,1)S(1)}, bf16[128,2048]{1,0:T(8,128)(2,1)S(1)}, u32[]{:S(2)}, u32[]{:S(2)}) collective-permute-start(bf16[128,2048]{1,0:T(8,128)(2,1)S(1)} %collective-permute-done.11.refs_0_.refs_2_), channel_id=1, source_target_pairs={{0,8},{8,16},{16,24},{24,0},{1,9},{9,17},{17,25},{25,1},{2,10},{10... | collective-permute-start | bytes 1572872 | tf_op jit(solution)/shard_map/ppermute | solution.py:252
  151.1 23.4 %collective-permute-start.20 = (bf16[64,3584]{1,0:T(8,128)(2,1)S(1)}, bf16[64,3584]{1,0:T(8,128)(2,1)S(1)}, u32[]{:S(2)}, u32[]{:S(2)}) collective-permute-start(bf16[64,3584]{1,0:T(8,128)(2,1)S(1)} %fusion.11), channel_id=1, source_target_pairs={{0,1},{1,0},{2,3},{3,2},{4,5},{5,4},{6,7},{7,6},{8,9},{9,8},{10,11... | collective-permute-start | bytes 1376264 | tf_op jit(solution)/shard_map/ppermute | solution.py:252
  151.7 21.4 %collective-permute-start.17 = (bf16[64,3584]{1,0:T(8,128)(2,1)S(1)}, bf16[64,3584]{1,0:T(8,128)(2,1)S(1)}, u32[]{:S(2)}, u32[]{:S(2)}) collective-permute-start(bf16[64,3584]{1,0:T(8,128)(2,1)S(1)} %fusion.11), channel_id=1, source_target_pairs={{0,4},{2,6},{4,0},{6,2},{1,5},{3,7},{5,1},{7,3},{8,12},{10,14},{12... | collective-permute-start | bytes 1376264 | tf_op jit(solution)/shard_map/ppermute | solution.py:252
  152.5 21.9 %collective-permute-start.15 = (bf16[128,2048]{1,0:T(8,128)(2,1)}, bf16[128,2048]{1,0:T(8,128)(2,1)S(1)}, u32[]{:S(2)}, u32[]{:S(2)}) collective-permute-start(bf16[128,2048]{1,0:T(8,128)(2,1)} %get-tuple-element.378), channel_id=1, source_target_pairs={{0,8},{8,16},{16,24},{24,0},{1,9},{9,17},{17,25},{25,1},{2,10},{10... | collective-permute-start | bytes 1572872 | tf_op jit(solution)/shard_map/ppermute | solution.py:252
  173.1 22.4 %collective-permute-start.22 = (bf16[64,3584]{1,0:T(8,128)(2,1)S(1)}, bf16[64,3584]{1,0:T(8,128)(2,1)}, u32[]{:S(2)}, u32[]{:S(2)}) collective-permute-start(bf16[64,3584]{1,0:T(8,128)(2,1)S(1)} %fusion.17), channel_id=1, source_target_pairs={{0,4},{2,6},{4,0},{6,2},{1,5},{3,7},{5,1},{7,3},{8,12},{10,14},{12... | collective-permute-start | bytes 1376264 | tf_op jit(solution)/shard_map/ppermute | solution.py:252
  174.6 23.0 %collective-permute-start.21 = (bf16[128,2048]{1,0:T(8,128)(2,1)S(1)}, bf16[128,2048]{1,0:T(8,128)(2,1)S(1)}, u32[]{:S(2)}, u32[]{:S(2)}) collective-permute-start(bf16[128,2048]{1,0:T(8,128)(2,1)S(1)} %copy-done.1), channel_id=1, source_target_pairs={{0,1},{1,0},{2,3},{3,2},{4,5},{5,4},{6,7},{7,6},{8,9},{9,8},{10,11... | collective-permute-start | bytes 1572872 | tf_op jit(solution)/shard_map/ppermute | solution.py:252
  176.2 21.4 %collective-permute-start.19 = (bf16[128,2048]{1,0:T(8,128)(2,1)S(1)}, bf16[128,2048]{1,0:T(8,128)(2,1)S(1)}, u32[]{:S(2)}, u32[]{:S(2)}) collective-permute-start(bf16[128,2048]{1,0:T(8,128)(2,1)S(1)} %add_convert_fusion.5), channel_id=1, source_target_pairs={{0,8},{8,16},{16,24},{24,0},{1,9},{9,17},{17,25},{25,1},{2,10},{10... | collective-permute-start | bytes 1572872 | tf_op jit(solution)/shard_map/ppermute | solution.py:252
  198.3 30.9 %collective-permute-start.23 = (bf16[128,2048]{1,0:T(8,128)(2,1)S(1)}, bf16[128,2048]{1,0:T(8,128)(2,1)S(1)}, u32[]{:S(2)}, u32[]{:S(2)}) collective-permute-start(bf16[128,2048]{1,0:T(8,128)(2,1)S(1)} %add_convert_fusion.4), channel_id=1, source_target_pairs={{0,8},{8,16},{16,24},{24,0},{1,9},{9,17},{17,25},{25,1},{2,10},{10... | collective-permute-start | bytes 1572872 | tf_op jit(solution)/shard_map/ppermute | solution.py:252
  209.9 33.3 %collective-permute-start.27 = (bf16[128,2048]{1,0:T(8,128)(2,1)S(1)}, bf16[128,2048]{1,0:T(8,128)(2,1)S(1)}, u32[]{:S(2)}, u32[]{:S(2)}) collective-permute-start(bf16[128,2048]{1,0:T(8,128)(2,1)S(1)} %copy-done.7), channel_id=1, source_target_pairs={{0,1},{1,0},{2,3},{3,2},{4,5},{5,4},{6,7},{7,6},{8,9},{9,8},{10,11... | collective-permute-start | bytes 1572872 | tf_op jit(solution)/shard_map/ppermute | solution.py:252
  230.1 15.8 %collective-permute-start.26 = (bf16[128,2048]{1,0:T(8,128)(2,1)S(1)}, bf16[128,2048]{1,0:T(8,128)(2,1)S(1)}, u32[]{:S(2)}, u32[]{:S(2)}) collective-permute-start(bf16[128,2048]{1,0:T(8,128)(2,1)S(1)} %copy-done.44), channel_id=1, source_target_pairs={{0,8},{8,16},{16,24},{24,0},{1,9},{9,17},{17,25},{25,1},{2,10},{10... | collective-permute-start | bytes 1572872 | tf_op jit(solution)/shard_map/ppermute | solution.py:252
  243.3 14.7 %collective-permute-start.32 = (bf16[128,2048]{1,0:T(8,128)(2,1)S(1)}, bf16[128,2048]{1,0:T(8,128)(2,1)S(1)}, u32[]{:S(2)}, u32[]{:S(2)}) collective-permute-start(bf16[128,2048]{1,0:T(8,128)(2,1)S(1)} %copy-done.9), channel_id=1, source_target_pairs={{0,1},{1,0},{2,3},{3,2},{4,5},{5,4},{6,7},{7,6},{8,9},{9,8},{10,11... | collective-permute-start | bytes 1572872 | tf_op jit(solution)/shard_map/ppermute | solution.py:252
  246.1 15.0 %collective-permute-start.29 = (bf16[128,2048]{1,0:T(8,128)(2,1)S(1)}, bf16[128,2048]{1,0:T(8,128)(2,1)S(1)}, u32[]{:S(2)}, u32[]{:S(2)}) collective-permute-start(bf16[128,2048]{1,0:T(8,128)(2,1)S(1)} %add_convert_fusion.2), channel_id=1, source_target_pairs={{0,8},{8,16},{16,24},{24,0},{1,9},{9,17},{17,25},{25,1},{2,10},{10... | collective-permute-start | bytes 1572872 | tf_op jit(solution)/shard_map/ppermute | solution.py:252
  258.1 14.2 %collective-permute-start.35 = (bf16[128,2048]{1,0:T(8,128)(2,1)S(1)}, bf16[128,2048]{1,0:T(8,128)(2,1)S(1)}, u32[]{:S(2)}, u32[]{:S(2)}) collective-permute-start(bf16[128,2048]{1,0:T(8,128)(2,1)S(1)} %copy-done.11), channel_id=1, source_target_pairs={{0,1},{1,0},{2,3},{3,2},{4,5},{5,4},{6,7},{7,6},{8,9},{9,8},{10,11... | collective-permute-start | bytes 1572872 | tf_op jit(solution)/shard_map/ppermute | solution.py:252
  261.3 37.2 %collective-permute-start.34 = (bf16[128,2048]{1,0:T(8,128)(2,1)S(1)}, bf16[128,2048]{1,0:T(8,128)(2,1)S(1)}, u32[]{:S(2)}, u32[]{:S(2)}) collective-permute-start(bf16[128,2048]{1,0:T(8,128)(2,1)S(1)} %add_convert_fusion.1), channel_id=1, source_target_pairs={{0,8},{8,16},{16,24},{24,0},{1,9},{9,17},{17,25},{25,1},{2,10},{10... | collective-permute-start | bytes 1572872 | tf_op jit(solution)/shard_map/ppermute | solution.py:252
  272.3 27.7 %collective-permute-start.39 = (bf16[64,3584]{1,0:T(8,128)(2,1)S(1)}, bf16[64,3584]{1,0:T(8,128)(2,1)S(1)}, u32[]{:S(2)}, u32[]{:S(2)}) collective-permute-start(bf16[64,3584]{1,0:T(8,128)(2,1)S(1)} %collective-permute-done.20.refs_10_), channel_id=1, source_target_pairs={{0,2},{2,0},{4,6},{6,4},{1,3},{3,1},{5,7},{7,5},{8,10},{10,8},{12,... | collective-permute-start | bytes 1376264 | tf_op jit(solution)/shard_map/ppermute | solution.py:252
  272.3 27.1 %collective-permute-start.40 = (bf16[64,3584]{1,0:T(8,128)(2,1)S(1)}, bf16[64,3584]{1,0:T(8,128)(2,1)S(1)}, u32[]{:S(2)}, u32[]{:S(2)}) collective-permute-start(bf16[64,3584]{1,0:T(8,128)(2,1)S(1)} %collective-permute-done.25.refs_14_), channel_id=1, source_target_pairs={{0,4},{2,6},{4,0},{6,2},{1,5},{3,7},{5,1},{7,3},{8,12},{10,14},{12... | collective-permute-start | bytes 1376264 | tf_op jit(solution)/shard_map/ppermute | solution.py:252
  274.4 25.6 %collective-permute-start.41 = (bf16[64,3584]{1,0:T(8,128)(2,1)S(1)}, bf16[64,3584]{1,0:T(8,128)(2,1)S(1)}, u32[]{:S(2)}, u32[]{:S(2)}) collective-permute-start(bf16[64,3584]{1,0:T(8,128)(2,1)S(1)} %collective-permute-done.36.refs_11_), channel_id=1, source_target_pairs={{0,2},{2,0},{4,6},{6,4},{1,3},{3,1},{5,7},{7,5},{8,10},{10,8},{12,... | collective-permute-start | bytes 1376264 | tf_op jit(solution)/shard_map/ppermute | solution.py:252
  (57 other events, 884.3 us)
